TPU v7x, 32 devices: a whole 2x2x4 slice. The times are simulated.
32 devices in a mesh: dp: 8 (over z, y), head: 4 (over x, core).
Axes of the slice: x: 2, y: 2, z: 4, core: 2. Of those that a mesh axis runs over, the one named last changes fastest.
Arguments:
- queries: bfloat16 [8192, 4096], P('dp', 'head'), may hold values from -6 to 6
- keys: bfloat16 [8192, 4096], P('dp', 'head'), may hold values from -6 to 6
- values: bfloat16 [8192, 4096], P('dp', 'head'), may hold values from -100 to 100
- out_grad: bfloat16 [8192, 4096], P('dp', 'head'), may hold values from -6 to 6
- norm_gain: float32 [4096], P('head'), may hold values from 0.1 to 1.9
- decay_table: float32 [16, 8], P('head'), may hold values from 0 to 0.52, as said below
- decay_index: int32 [16, 8192], P('head', 'dp'), may hold values from 0 to 7
- rollout_lengths: int32 [6], replicated, may hold values from 1 to 4096, 8192 in all
- move_partner: int32 [8], replicated, may hold values from 0 to 7, as said below
- move_slot: int32 [8], replicated, may hold values from 0 to 31, as said below
Outputs:
- query_grad: bfloat16 [8192, 4096], P('dp', 'head')
- key_grad: bfloat16 [8192, 4096], P('dp', 'head')
- value_grad: bfloat16 [8192, 4096], P('dp', 'head')
Inputs may be any that keep to these rules, and one draw needn't show every extreme that they name: `decay_table`: positive rates. `rollout_lengths`: they sum to 8192. move_partner[d] is either d itself or a row whose index differs from d in exactly one bit, and the partner of the partner is the row itself. `move_slot`: one block of each row.
All inputs are finite; a program needn't handle non-finite values.
Results may differ from a plain program's by a relative error of at most 0.0063.
Values may be sent and summed in bfloat16 or wider, within the bound.
A program may use at most 128 MiB of HBM per device.

v0:
```python
import functools

import jax
import jax.numpy as jnp
from jax import lax
from jax.experimental import pallas as pl
from jax.experimental.pallas import tpu as pltpu
from jax.sharding import PartitionSpec as P

HEAD_DIM = 256
BLOCK_LEN = 32
FEATURES = 4096
EPSILON = 1e-05
TILE = 256
MESH = pl.DeviceIdType.MESH
F32 = jnp.float32
BF16 = jnp.bfloat16


def dot_nt(a, b):
    return lax.dot_general(a, b, (((1,), (1,)), ((), ())), preferred_element_type=F32)


def dot_tn(a, b):
    return lax.dot_general(a, b, (((0,), (0,)), ((), ())), preferred_element_type=F32)


def dot_nn(a, b):
    return jnp.dot(a, b, preferred_element_type=F32)


def twice(col):
    return jnp.concatenate([col, col], axis=1)


def to_column(row, tokens):
    return jnp.transpose(jnp.broadcast_to(row, (128, tokens)))


def main_kernel(
    count, hcount, heads, tokens,
    lengths, partners, slots, table, index, gain, q_hbm, k_hbm, v_hbm, dy_hbm,
    pdy, pk, pv, guest_out,
    pq, wts, decay, gw, ret, dkin, grad, colb, segc, cum_s,
    sel, unsel, guest_kv, last_g, fin, bstate, rate_out, rate_in, blk_out, blk_in, w_in, w_out,
    st_out, st_in, st_ret, carry, bk_in, bk_ret, cback, mid_out, mid_in,
    hs_out, hs_in, lv_out, lv_in,
    in_sem, rate_ss, rate_rs, blk_ss, blk_rs, w_ss, w_rs,
    p1_ss, p1_rs, p2_ss, p2_rs, b1_ss, b1_rs, b2_ss, b2_rs, mid_ss, mid_rs, hs_ss, hs_rs, lv_ss, lv_rs,
):
    me = lax.axis_index("dp")
    hme = lax.axis_index("head")
    levels = count.bit_length() - 1
    length = BLOCK_LEN
    group = count // 2
    side = me // group
    base_row = side * group
    pos = me - base_row
    mate = me + group - 2 * group * side
    span = heads * HEAD_DIM // group
    sub_span = span // 2
    tiles = tokens // TILE
    width = heads * HEAD_DIM
    inv = 1.0 / HEAD_DIM

    loads = []
    for i, (src, dst) in enumerate(((k_hbm, pk), (v_hbm, pv), (q_hbm, pq), (dy_hbm, pdy))):
        copy = pltpu.make_async_copy(src, dst, in_sem.at[i])
        copy.start()
        loads.append(copy)

    barrier = pltpu.get_barrier_semaphore()
    for o in range(1, count):
        pl.semaphore_signal(barrier, inc=1, device_id={"dp": lax.rem(me + o, count)}, device_id_type=MESH)
    for o in range(1, hcount):
        pl.semaphore_signal(barrier, inc=1, device_id={"head": lax.rem(hme + o, hcount)}, device_id_type=MESH)

    idx = index[...]
    rate = jnp.zeros((heads, tokens), F32)
    for level in range(table.shape[1]):
        rate = jnp.where(idx == level, table[:, level:level + 1], rate)
    rate_out[...] = jnp.zeros((8, tokens), F32)
    rate_out[0:heads, :] = rate

    slot = slots[me]
    partner = partners[me]
    partner_slot = slot
    for d in range(count):
        partner_slot = jnp.where(partner == d, slots[d], partner_slot)
    pl.semaphore_wait(barrier, count - 1 + hcount - 1)

    def remote(src, dst, ss, rs, axis, to):
        return pltpu.make_async_remote_copy(
            src_ref=src, dst_ref=dst, send_sem=ss, recv_sem=rs,
            device_id={axis: to}, device_id_type=MESH,
        )

    def other(level):
        bit = 1 << level
        return me + bit - 2 * bit * (lax.rem(me // bit, 2))

    rate_copies = []
    for level in range(levels):
        copy = remote(rate_out, rate_in.at[level], rate_ss.at[level], rate_rs.at[level], "dp", other(level))
        copy.start()
        rate_copies.append(copy)

    blocks = tokens // length

    chosen = lax.broadcasted_iota(jnp.int32, (tokens, 128), 0) // length == jnp.full((tokens, 128), slot, jnp.int32)
    sel[...] = jnp.where(chosen, 1.0, 0.0).astype(BF16)
    unsel[...] = jnp.where(chosen, 0.0, 1.0).astype(BF16)

    def widen(mask):
        return jnp.concatenate([mask] * (width // 128), axis=1)

    def pick(ref):
        def one(b, acc):
            at = pl.ds(pl.multiple_of(b * length, length), length)
            return acc + ref[at, :] * widen(sel[at, :])

        return lax.fori_loop(0, blocks, one, jnp.zeros((length, width), BF16))

    def to_partners(out, inbox, ss, rs, first):
        copies = []
        for level in range(levels):
            copy = remote(out, inbox(level), ss.at[first + level], rs.at[first + level], "dp", other(level))
            copy.start()
            copies.append(copy)
        return copies

    def guest_of(own_block, inbox):
        block = own_block.astype(F32)
        for level in range(levels):
            match = jnp.full(block.shape, partner, jnp.int32) == other(level)
            block = jnp.where(match, inbox(level).astype(F32), block)
        return block.astype(BF16)

    def put(ref, block):
        def one(b, _):
            at = pl.ds(pl.multiple_of(b * length, length), length)
            ref[at, :] = ref[at, :] * widen(unsel[at, :]) + block * widen(sel[at, :])
            return 0

        lax.fori_loop(0, blocks, one, 0)

    packed = (pk, pv, pq, pdy)

    def load_and_pick(i):
        loads[i].wait()
        blk_out[i] = pick(packed[i])

    load_and_pick(0)
    load_and_pick(1)
    kv_copies = to_partners(blk_out.at[0:2], lambda level: blk_in.at[level, 0:2], blk_ss, blk_rs, 0)
    load_and_pick(2)
    q_copies = to_partners(blk_out.at[2], lambda level: blk_in.at[level, 2], blk_ss, blk_rs, levels)
    load_and_pick(3)

    lane = lax.broadcasted_iota(jnp.int32, (8, tokens), 1)
    sub = lax.broadcasted_iota(jnp.int32, (8, tokens), 0)
    flag = jnp.zeros((8, tokens), F32)
    start = jnp.int32(0)
    for n in range(lengths.shape[0]):
        flag = jnp.where(lane == start - me * tokens, 1.0, flag)
        start = start + lengths[n]

    own = rate_out[...]
    guest = own
    for level in range(levels):
        rate_copies[level].wait()
        guest = jnp.where(jnp.full((8, tokens), partner, jnp.int32) == other(level), rate_in[level], guest)
    shift = slot - partner_slot + blocks
    for bit in range(blocks.bit_length() - 1):
        here = (jnp.full((8, tokens), shift, jnp.int32) >> bit) & 1
        guest = jnp.where(here == 1, pltpu.roll(guest, length << bit, 1), guest)
    rows = jnp.where(lane // length == jnp.full((8, tokens), slot, jnp.int32), guest, own)
    cum = jnp.where(sub == heads, flag, rows)
    step = 1
    while step < tokens:
        cum = cum + jnp.where(lane >= step, pltpu.roll(cum, step, 1), 0.0)
        step *= 2
    cum_s[...] = cum
    seg = cum[heads:heads + 1, :]
    seg_last = cum[heads:heads + 1, tokens - 1:tokens]
    cum_last = cum[:, tokens - 1:tokens]
    first8 = jnp.where(seg == 0.0, jnp.exp(-cum), 0.0)
    last8 = jnp.where(seg == seg_last, jnp.exp(cum - cum_last), 0.0)
    whole8 = jnp.where(seg_last == 0.0, jnp.exp(-cum_last), 0.0)
    w_out[...] = jnp.broadcast_to(whole8, (8, 128))
    w_copies = []
    for o in range(1, count):
        to = lax.rem(me + o, count)
        copy = remote(w_out, w_in.at[me], w_ss.at[o], w_rs.at[me], "dp", to)
        copy.start()
        w_copies.append(copy)
    w_in[me] = w_out[...]
    for h in range(heads):
        colb[h] = to_column(cum[h:h + 1, :], tokens)
        colb[heads + h] = to_column(first8[h:h + 1, :], tokens)
        colb[2 * heads + h] = to_column(last8[h:h + 1, :], tokens)
    segc[...] = to_column(seg, tokens)

    def columns(h):
        return pl.ds(pl.multiple_of(h * HEAD_DIM, HEAD_DIM), HEAD_DIM)

    def state_rows(h):
        return pl.ds(pl.multiple_of(h * HEAD_DIM, HEAD_DIM), HEAD_DIM)

    def span_rows(j):
        return pl.ds(pl.multiple_of(j * span, span), span)

    def part_rows(j, c):
        return pl.ds(pl.multiple_of(j * span + c * sub_span, sub_span), sub_span)

    def half_rows(c):
        return pl.ds(c * sub_span, sub_span)

    def scatter(inbox, ss, rs, c):
        copies = []
        for o in range(1, group):
            to = lax.rem(pos + o, group)
            copy = remote(
                st_out.at[part_rows(to, c)], inbox.at[pos, half_rows(c)],
                ss.at[c * group + o], rs.at[c * group + pos], "dp", base_row + to,
            )
            copy.start()
            copies.append(copy)
        inbox[pos, half_rows(c), :] = st_out[part_rows(pos, c), :]
        return copies

    head_of_span = pos * span // HEAD_DIM

    def fold(inbox, run, reverse, outbox, c):
        def one(turn, run):
            d = group - 1 - turn if reverse else turn
            if outbox is not None:
                outbox[d, half_rows(c), :] = run.astype(BF16)
            w = w_in[base_row + d, pl.ds(head_of_span, 1), :]
            return twice(w) * run + inbox[d, half_rows(c), :].astype(F32)

        return lax.fori_loop(0, group, one, run)

    def across(inbox, rs, ss, which, reverse, c):
        for o in range(1, group):
            frm = lax.rem(pos + group - o, group)
            remote(
                st_out.at[part_rows(0, c)], inbox.at[frm, half_rows(c)],
                ss.at[c * group + o], rs.at[c * group + frm], "dp", base_row + frm,
            ).wait_recv()
        at = 2 * which + c
        mid_out[at] = fold(inbox, jnp.zeros((sub_span, HEAD_DIM), F32), reverse, None, c).astype(BF16)
        copy = remote(mid_out.at[at], mid_in.at[at], mid_ss.at[at], mid_rs.at[at], "dp", mate)
        copy.start()
        return copy

    def prefix(inbox, outbox, home, ss2, rs2, which, copy, reverse, c):
        copy.wait_recv()
        behind = jnp.full((sub_span, HEAD_DIM), side, jnp.int32) == (0 if reverse else 1)
        run = jnp.where(behind, mid_in[2 * which + c].astype(F32), 0.0)
        fold(inbox, run, reverse, outbox, c)
        copies = []
        for o in range(1, group):
            to = lax.rem(pos + o, group)
            out = remote(
                outbox.at[to, half_rows(c)], home.at[part_rows(pos, c)],
                ss2.at[c * group + o], rs2.at[c * group + pos], "dp", base_row + to,
            )
            out.start()
            copies.append(out)
        home[part_rows(pos, c), :] = outbox[pos, half_rows(c), :]
        return copies

    def gather_wait(home, outbox, ss2, rs2):
        for c in range(2):
            for o in range(1, group):
                frm = lax.rem(pos + group - o, group)
                remote(
                    outbox.at[0, half_rows(c)], home.at[part_rows(frm, c)],
                    ss2.at[c * group + o], rs2.at[c * group + frm], "dp", base_row + frm,
                ).wait_recv()

    def kept_state(h, _):
        last = colb[2 * heads + h]
        gated = (pv[:, columns(h)].astype(F32) * twice(last)).astype(BF16) * twice(unsel[...])
        dkin[state_rows(h), 0:HEAD_DIM] = dot_tn(pk[:, columns(h)], gated)

        def one(b, acc):
            at = pl.ds(pl.multiple_of(b * length, length), length)
            return acc + colb[2 * heads + h, at, :] * sel[at, :].astype(F32)

        last_g[h] = lax.fori_loop(0, blocks, one, jnp.zeros((length, 128), F32))
        return 0

    lax.fori_loop(0, heads, kept_state, 0)

    def make_decay(h, _):
        for tb in range(tiles):
            base = tb * (tb + 1) // 2 * TILE
            trow = pl.ds(tb * TILE, TILE)
            ct = twice(colb[h, trow, :])
            sc = twice(segc[trow, :])
            for sb in range(tb + 1):
                scol = pl.ds(sb * TILE, TILE)
                inside = cum_s[heads:heads + 1, scol] == sc
                if sb == tb:
                    r = lax.broadcasted_iota(jnp.int32, (TILE, TILE), 0)
                    c = lax.broadcasted_iota(jnp.int32, (TILE, TILE), 1)
                    inside = inside & (r >= c)
                value = jnp.exp(jnp.minimum(cum_s[pl.ds(h, 1), scol] - ct, 0.0)) * inv
                decay[h, :, base + sb * TILE:base + (sb + 1) * TILE] = jnp.where(inside, value, 0.0)
        return 0

    cuts = [heads * i // 4 for i in range(5)]
    for copy in kv_copies:
        copy.wait()
    for i in range(2):
        guest_kv[i] = guest_of(blk_out[i], lambda level: blk_in[level, i])

    def local_state(h, _):
        gated = (guest_kv[1, :, columns(h)].astype(F32) * twice(last_g[h])).astype(BF16)
        state = dkin[state_rows(h), 0:HEAD_DIM] + dot_tn(guest_kv[0, :, columns(h)], gated)
        st_out[state_rows(h), :] = state.astype(BF16)
        return 0

    lax.fori_loop(0, heads, local_state, 0)
    p1 = scatter(st_in, p1_ss, p1_rs, 0) + scatter(st_in, p1_ss, p1_rs, 1)
    dy_copies = to_partners(blk_out.at[3], lambda level: blk_in.at[level, 3], blk_ss, blk_rs, 2 * levels)
    lax.fori_loop(cuts[0], cuts[2], make_decay, 0)
    put(pk, guest_kv[0])
    put(pv, guest_kv[1])
    for copy in q_copies:
        copy.wait()
    put(pq, guest_of(blk_out[2], lambda level: blk_in[level, 2]))

    def forward(h, _):
        cols = columns(h)
        for tb in range(tiles):
            n = (tb + 1) * TILE
            base = tb * (tb + 1) // 2 * TILE
            trow = pl.ds(tb * TILE, TILE)
            scores = dot_nt(pq[trow, cols], pk[0:n, cols])
            w = (scores * decay[h, :, base:base + n]).astype(BF16)
            wts[h, trow, 0:n] = w
            ret[trow, cols] = dot_nn(w, pv[0:n, cols])
        return 0

    lax.fori_loop(cuts[0], cuts[1], forward, 0)
    for o in range(1, count):
        w_copies[o - 1].wait_send()
        frm = lax.rem(me + count - o, count)
        remote(w_out, w_in.at[frm], w_ss.at[o], w_rs.at[frm], "dp", frm).wait_recv()
    mid = [across(st_in, p1_rs, p1_ss, 0, False, 0)]
    lax.fori_loop(cuts[2], cuts[4], make_decay, 0)
    lax.fori_loop(cuts[1], cuts[2], forward, 0)
    mid.append(across(st_in, p1_rs, p1_ss, 0, False, 1))
    lax.fori_loop(cuts[2], cuts[3], forward, 0)
    p2 = prefix(st_in, st_ret, carry, p2_ss, p2_rs, 0, mid[0], False, 0)
    lax.fori_loop(cuts[3], cuts[4], forward, 0)
    p2 += prefix(st_in, st_ret, carry, p2_ss, p2_rs, 0, mid[1], False, 1)
    for copy in dy_copies:
        copy.wait()
    put(pdy, guest_of(blk_out[3], lambda level: blk_in[level, 3]))
    gather_wait(carry, st_ret, p2_ss, p2_rs)

    half = tokens // 2
    halves = (pl.ds(0, half), pl.ds(half, half))
    h_copies = []

    def send_sums(part):
        rows = halves[part]

        def cross(h, sums):
            cols = columns(h)
            r = dot_nn(pq[rows, cols], carry[state_rows(h), :])
            r = ret[rows, cols] + r * (twice(colb[heads + h, rows, :]) * inv)
            ret[rows, cols] = r
            s = gain[:, cols] * pdy[rows, cols].astype(F32)
            sq = r * r
            sr = s * r
            return (sums[0] + sq[:, 0:128] + sq[:, 128:256], sums[1] + sr[:, 0:128] + sr[:, 128:256])

        zero = jnp.zeros((half, 128), F32)
        sums = lax.fori_loop(0, heads, cross, (zero, zero))
        sq_row = jnp.sum(jnp.transpose(sums[0]), axis=0, keepdims=True)
        in_row = jnp.sum(jnp.transpose(sums[1]), axis=0, keepdims=True)
        top = lax.broadcasted_iota(jnp.int32, (8, half), 0) == 0
        hs_out[part] = jnp.where(top, sq_row, in_row)
        for o in range(1, hcount):
            to = lax.rem(hme + o, hcount)
            at = part * hcount
            copy = remote(
                hs_out.at[part], hs_in.at[part, hme], hs_ss.at[at + o], hs_rs.at[at + hme], "head", to
            )
            copy.start()
            h_copies.append(copy)

    def norm_columns(part):
        rows = halves[part]
        both = hs_out[part]
        for o in range(1, hcount):
            frm = lax.rem(hme + hcount - o, hcount)
            at = part * hcount
            remote(
                hs_out.at[part], hs_in.at[part, frm], hs_ss.at[at + o], hs_rs.at[at + frm], "head", frm
            ).wait_recv()
            both = both + hs_in[part, frm]
        recip = lax.rsqrt(both[0:1, :] * (1.0 / FEATURES) + EPSILON)
        coef = recip * recip * recip * both[1:2, :] * (1.0 / FEATURES)
        segc[rows, :] = to_column(recip, half)
        dkin[rows, 0:128] = to_column(coef, half)

    def back_state(part):
        rows = halves[part]

        def one(h, _):
            cols = columns(h)
            s = gain[:, cols] * pdy[rows, cols].astype(F32)
            g = (twice(segc[rows, :]) * s - twice(dkin[rows, 0:128]) * ret[rows, cols]).astype(BF16)
            grad[rows, cols] = g
            gated = (g.astype(F32) * twice(colb[heads + h, rows, :])).astype(BF16)
            state = dot_tn(pq[rows, cols], gated)
            if part == 0:
                bstate[state_rows(h), :] = state
            else:
                st_out[state_rows(h), :] = ((bstate[state_rows(h), :] + state) * inv).astype(BF16)
            return 0

        lax.fori_loop(0, heads, one, 0)

    send_sums(0)
    send_sums(1)
    for copy in p1:
        copy.wait_send()
    norm_columns(0)
    back_state(0)
    norm_columns(1)
    back_state(1)
    b1 = scatter(bk_in, b1_ss, b1_rs, 0) + scatter(bk_in, b1_ss, b1_rs, 1)

    def backward(h, _):
        cols = columns(h)
        for tb in range(tiles):
            n = (tb + 1) * TILE
            base = tb * (tb + 1) // 2 * TILE
            trow = pl.ds(tb * TILE, TILE)
            g = grad[trow, cols]
            scores = dot_nt(g, pv[0:n, cols])
            w = (scores * decay[h, :, base:base + n]).astype(BF16)
            gw[trow, 0:n] = w
            part = dot_nt(g, carry[state_rows(h), :])
            fc = twice(colb[heads + h, trow, :]) * inv
            pdy[trow, cols] = (dot_nn(w, pk[0:n, cols]) + fc * part).astype(BF16)
        for sb in range(tiles):
            lo = sb * TILE
            srow = pl.ds(lo, TILE)
            dkin[srow, cols] = dot_tn(gw[lo:, lo:lo + TILE], pq[lo:, cols])
            ret[srow, cols] = dot_tn(wts[h, lo:, lo:lo + TILE], grad[lo:, cols])
        return 0

    lax.fori_loop(cuts[0], cuts[1], backward, 0)
    back_mid = [across(bk_in, b1_rs, b1_ss, 1, True, 0)]
    lax.fori_loop(cuts[1], cuts[2], backward, 0)
    back_mid.append(across(bk_in, b1_rs, b1_ss, 1, True, 1))
    lax.fori_loop(cuts[2], cuts[3], backward, 0)
    b2 = prefix(bk_in, bk_ret, cback, b2_ss, b2_rs, 1, back_mid[0], True, 0)
    b2 += prefix(bk_in, bk_ret, cback, b2_ss, b2_rs, 1, back_mid[1], True, 1)
    lax.fori_loop(cuts[3], cuts[4], backward, 0)
    lv_out[0] = pick(pdy)
    lv_copies = to_partners(lv_out.at[0], lambda level: lv_in.at[level, 0], lv_ss, lv_rs, 0)

    def pick_wide(b, acc):
        at = pl.ds(pl.multiple_of(b * length, length), length)
        mask = widen(sel[at, :].astype(F32))
        return acc[0] + dkin[at, :] * mask, acc[1] + ret[at, :] * mask

    zero = jnp.zeros((length, width), F32)
    fin[0], fin[1] = lax.fori_loop(0, blocks, pick_wide, (zero, zero))
    gather_wait(cback, bk_ret, b2_ss, b2_rs)

    def finish_block(h, _):
        cols = columns(h)
        lc = twice(last_g[h])
        state = cback[state_rows(h), :]
        lv_out[1, :, cols] = (fin[0, :, cols] + lc * dot_nt(guest_kv[1, :, cols], state)).astype(BF16)
        lv_out[2, :, cols] = (fin[1, :, cols] + lc * dot_nn(guest_kv[0, :, cols], state)).astype(BF16)
        return 0

    lax.fori_loop(0, heads, finish_block, 0)
    lv_copies += to_partners(lv_out.at[1:3], lambda level: lv_in.at[level, 1:3], lv_ss, lv_rs, levels)

    def finish(h, _):
        cols = columns(h)
        lc = twice(colb[2 * heads + h])
        state = cback[state_rows(h), :]
        k = pk[:, cols]
        dk = dkin[:, cols] + lc * dot_nt(pv[:, cols], state)
        dv = ret[:, cols] + lc * dot_nn(k, state)
        pk[:, cols] = dk.astype(BF16)
        pv[:, cols] = dv.astype(BF16)
        return 0

    lax.fori_loop(0, heads, finish, 0)
    for copy in p2 + b1 + b2 + h_copies + mid + back_mid:
        copy.wait_send()
    for copy in lv_copies:
        copy.wait()
    for i in range(3):
        guest_out[i] = guest_of(lv_out[i], lambda level: lv_in[level, i])


def place_kernel(slots, guest, dq, dk, dv, oq, ok, ov, sem):
    slot = slots[lax.axis_index("dp")]
    per = 4
    chunk = per * BLOCK_LEN

    def one(c, _):
        inside = slot // per == c
        at = pl.multiple_of(c * chunk, chunk)
        for i, (src, dst) in enumerate(((dq, oq), (dk, ok), (dv, ov))):

            @pl.when(jnp.logical_not(inside))
            def _():
                rows = pl.ds(at, chunk)
                pltpu.make_async_copy(src.at[rows], dst.at[rows], sem.at[i]).start()

            @pl.when(inside)
            def _():
                for b in range(per):
                    rows = pl.ds(pl.multiple_of(at + b * BLOCK_LEN, BLOCK_LEN), BLOCK_LEN)

                    @pl.when(c * per + b == slot)
                    def _():
                        pltpu.make_async_copy(guest.at[i], dst.at[rows], sem.at[i]).start()

                    @pl.when(c * per + b != slot)
                    def _():
                        pltpu.make_async_copy(src.at[rows], dst.at[rows], sem.at[i]).start()

        return 0

    lax.fori_loop(0, dq.shape[0] // chunk, one, 0)
    for i, (src, dst) in enumerate(((dq, oq), (dk, ok), (dv, ov))):
        pltpu.make_async_copy(src, dst, sem.at[i]).wait()


def local(count, hcount, queries, keys, values, out_grad, norm_gain, table, index, lengths, partners, slots):
    tokens, width = queries.shape
    heads = table.shape[0]
    tiles = tokens // TILE
    levels = count.bit_length() - 1
    group = count // 2
    span = heads * HEAD_DIM // group
    smem = pl.BlockSpec(memory_space=pltpu.SMEM)
    vmem = pl.BlockSpec(memory_space=pltpu.VMEM)
    any_ = pl.BlockSpec(memory_space=pl.ANY)
    full = jax.ShapeDtypeStruct((tokens, width), BF16)
    V = pltpu.VMEM
    D = pltpu.SemaphoreType.DMA
    held = V((tokens, width), BF16)
    state = V((heads * HEAD_DIM, HEAD_DIM), BF16)
    part = V((group, span, HEAD_DIM), BF16)
    dq, dk, dv, guest = pl.pallas_call(
        functools.partial(main_kernel, count, hcount, heads, tokens),
        out_shape=(held, held, held, V((3, BLOCK_LEN, width), BF16)),
        in_specs=[smem, smem, smem, vmem, vmem, vmem, any_, any_, any_, any_],
        out_specs=(vmem, vmem, vmem, vmem),
        scratch_shapes=[
            held,
            V((heads, tokens, tokens), BF16),
            V((heads, TILE, tiles * (tiles + 1) // 2 * TILE), F32),
            V((tokens, tokens), BF16),
            V((tokens, width), F32), V((tokens, width), F32), V((tokens, width), BF16),
            V((3 * heads, tokens, 128), F32), V((tokens, 128), F32), V((8, tokens), F32),
            V((tokens, 128), BF16), V((tokens, 128), BF16),
            V((2, BLOCK_LEN, width), BF16), V((heads, BLOCK_LEN, 128), F32), V((2, BLOCK_LEN, width), F32),
            V((heads * HEAD_DIM, HEAD_DIM), F32),
            V((8, tokens), F32), V((levels, 8, tokens), F32),
            V((4, BLOCK_LEN, width), BF16), V((levels, 4, BLOCK_LEN, width), BF16),
            V((count, 8, 128), F32), V((8, 128), F32),
            state, part, part, state, part, part, state,
            V((4, span // 2, HEAD_DIM), BF16), V((4, span // 2, HEAD_DIM), BF16),
            V((2, 8, tokens // 2), F32), V((2, hcount, 8, tokens // 2), F32),
            V((3, BLOCK_LEN, width), BF16), V((levels, 3, BLOCK_LEN, width), BF16),
            D((4,)), D((levels,)), D((levels,)), D((3 * levels,)), D((3 * levels,)),
            D((count,)), D((count,)), D((2 * group,)), D((2 * group,)), D((2 * group,)), D((2 * group,)),
            D((2 * group,)), D((2 * group,)), D((2 * group,)), D((2 * group,)), D((4,)), D((4,)),
            D((2 * hcount,)), D((2 * hcount,)), D((2 * levels,)), D((2 * levels,)),
        ],
        compiler_params=pltpu.CompilerParams(
            collective_id=0, has_side_effects=True, vmem_limit_bytes=50 * 1024 * 1024
        ),
    )(lengths, partners, slots, table, index, norm_gain.reshape(1, width), queries, keys, values, out_grad)

    kept = [pltpu.with_memory_space_constraint(a, pltpu.VMEM) for a in (guest, dq, dk, dv)]
    return pl.pallas_call(
        place_kernel,
        out_shape=(full, full, full),
        in_specs=[smem, vmem, vmem, vmem, vmem],
        out_specs=(any_, any_, any_),
        scratch_shapes=[D((3,))],
        compiler_params=pltpu.CompilerParams(vmem_limit_bytes=1024 * 1024),
    )(slots, *kept)


def solution(mesh):
    placed = (
        P("dp", "head"), P("dp", "head"), P("dp", "head"), P("dp", "head"),
        P("head"), P("head", None), P("head", "dp"), P(), P(), P(),
    )
    return jax.shard_map(
        functools.partial(local, mesh.shape["dp"], mesh.shape["head"]),
        mesh=mesh,
        in_specs=placed,
        out_specs=(P("dp", "head"), P("dp", "head"), P("dp", "head")),
        check_vma=False,
    )
```

profile of v0, /device:TPU:0, one launch (start us, length us, event | category | flops | bytes accessed | tf_op | source)
XLA Modules:
  0.0 77.7 jit_solution(10164087134038083286)
XLA Ops:
  0.6 0.0 copy-start
  0.6 73.6 %shard_map.121 = (bf16[1024,1024]{1,0:T(8,128)(2,1)S(1)}, bf16[1024,1024]{1,0:T(8,128)(2,1)S(1)}, bf16[1024,1024]{1,0:T(8,128)(2,1)S(1)}, bf16[3,32,1024]{2,1,0:T(8,128)(2,1)S(1)}) custom-call(s32[6]{0:T(128)} %lengths.1, s32[8]{0:T(128)} %partners.1, s32[8]{0:T(128)} %slots.3, f32[4,8]{1,0:T(4,128)} %table.1, s32[4,1024]{1,0:T(4,128)} %index.1, ...), custom_call_target="tpu_custom_call" | custom-call | tf_op jit(solution)/shard_map/pallas_call | solution.py:563
  74.3 0.0 copy-done
  74.3 3.2 %shard_map.122 = (bf16[1024,1024]{1,0:T(8,128)(2,1)}, bf16[1024,1024]{1,0:T(8,128)(2,1)}, bf16[1024,1024]{1,0:T(8,128)(2,1)}) custom-call(s32[8]{0:T(128)S(1)} %copy-done, bf16[3,32,1024]{2,1,0:T(8,128)(2,1)S(1)} %get-tuple-element.7.guest, bf16[1024,1024]{1,0:T(8,128)(2,1)S(1)} %get-tuple-element.8.dq, bf16[1024,1024]{1,0:T(8,128)(2,1)S(1)} %get-tuple-element.9.dk, ...), custom_call_target="tpu_custom_call" | custom-call | tf_op jit(solution)/shard_map/pallas_call | solution.py:596
Async XLA Ops:
  0.6 73.7 %copy-start = (s32[8]{0:T(128)S(1)}, s32[8]{0:T(128)}, u32[]{:S(2)}) copy-start(s32[8]{0:T(128)} %slots.3) | copy-start | bytes 100
where the time goes:
time: 77.8 us; the launch traced here: 77.7 us
  Pallas kernels  76.9 us (99%)
  between operations  0.82 us (1%)
    pallas_call x1, Pallas kernels, local(): pl.pallas_call(functools.partial(main_kernel, count, hcount, heads, token...  73.6 us
    pallas_call x1, Pallas kernels, local(): pl.pallas_call(place_kernel, out_shape=(full, full, full), in_specs=[smem...  3.22 us

commit v1 on v0

--- a/solution.py
+++ b/solution.py
@@ -196,10 +196,7 @@
         w_copies.append(copy)
     w_in[me] = w_out[...]
     for h in range(heads):
-        colb[h] = to_column(cum[h:h + 1, :], tokens)
-        colb[heads + h] = to_column(first8[h:h + 1, :], tokens)
         colb[2 * heads + h] = to_column(last8[h:h + 1, :], tokens)
-    segc[...] = to_column(seg, tokens)
 
     def columns(h):
         return pl.ds(pl.multiple_of(h * HEAD_DIM, HEAD_DIM), HEAD_DIM)
@@ -326,6 +323,10 @@
     lax.fori_loop(0, heads, local_state, 0)
     p1 = scatter(st_in, p1_ss, p1_rs, 0) + scatter(st_in, p1_ss, p1_rs, 1)
     dy_copies = to_partners(blk_out.at[3], lambda level: blk_in.at[level, 3], blk_ss, blk_rs, 2 * levels)
+    for h in range(heads):
+        colb[h] = to_column(cum[h:h + 1, :], tokens)
+        colb[heads + h] = to_column(first8[h:h + 1, :], tokens)
+    segc[...] = to_column(seg, tokens)
     lax.fori_loop(cuts[0], cuts[2], make_decay, 0)
     put(pk, guest_kv[0])
     put(pv, guest_kv[1])

time: 77.8 us -> 76.7 us (0.986)
  Pallas kernels: 76.9 us -> 75.6 us
    pallas_call x1, Pallas kernels: 73.6 us -> 72.4 us  [local(): pl.pallas_call(functools.partial(main_kernel, count, hcount, heads, token...]
where the time goes in v1:
time: 76.7 us; the launch traced here: 76.4 us
  Pallas kernels  75.6 us (99%)
  between operations  0.82 us (1%)
    pallas_call x1, Pallas kernels, local(): pl.pallas_call(functools.partial(main_kernel, count, hcount, heads, token...  72.4 us
    pallas_call x1, Pallas kernels, local(): pl.pallas_call(place_kernel, out_shape=(full, full, full), in_specs=[smem...  3.22 us

profile of v1, /device:TPU:0, one launch (start us, length us, event | category | flops | bytes accessed | tf_op | source)
XLA Modules:
  0.0 76.4 jit_solution(13805809711140183835)
XLA Ops:
  0.6 0.0 copy-start
  0.6 72.4 %shard_map.121 = (bf16[1024,1024]{1,0:T(8,128)(2,1)S(1)}, bf16[1024,1024]{1,0:T(8,128)(2,1)S(1)}, bf16[1024,1024]{1,0:T(8,128)(2,1)S(1)}, bf16[3,32,1024]{2,1,0:T(8,128)(2,1)S(1)}) custom-call(s32[6]{0:T(128)} %lengths.1, s32[8]{0:T(128)} %partners.1, s32[8]{0:T(128)} %slots.3, f32[4,8]{1,0:T(4,128)} %table.1, s32[4,1024]{1,0:T(4,128)} %index.1, ...), custom_call_target="tpu_custom_call" | custom-call | tf_op jit(solution)/shard_map/pallas_call | solution.py:564
  73.0 0.0 copy-done
  73.0 3.2 %shard_map.122 = (bf16[1024,1024]{1,0:T(8,128)(2,1)}, bf16[1024,1024]{1,0:T(8,128)(2,1)}, bf16[1024,1024]{1,0:T(8,128)(2,1)}) custom-call(s32[8]{0:T(128)S(1)} %copy-done, bf16[3,32,1024]{2,1,0:T(8,128)(2,1)S(1)} %get-tuple-element.7.guest, bf16[1024,1024]{1,0:T(8,128)(2,1)S(1)} %get-tuple-element.8.dq, bf16[1024,1024]{1,0:T(8,128)(2,1)S(1)} %get-tuple-element.9.dk, ...), custom_call_target="tpu_custom_call" | custom-call | tf_op jit(solution)/shard_map/pallas_call | solution.py:597
Async XLA Ops:
  0.6 72.4 %copy-start = (s32[8]{0:T(128)S(1)}, s32[8]{0:T(128)}, u32[]{:S(2)}) copy-start(s32[8]{0:T(128)} %slots.3) | copy-start | bytes 100
